TPU v7x, 768 devices: a whole 4x8x12 slice. The times are simulated.
768 devices in a mesh: row: 24 (over z_hi, y), col: 32 (over z_lo, x, core).
Axes of the slice: x: 4, y: 8, z: 12 (z_hi: 3, z_lo: 4; z = z_hi * 4 + z_lo), core: 2. Of those that a mesh axis runs over, the one named last changes fastest.
Arguments:
- density: float32 [1536, 9, 128, 128], P(('row', 'col')), may hold values from -0.1 to 0.6, as said below
- band_mask: int32 [1536, 9], P(('row', 'col')), may hold values 0 or 1
Outputs:
- purified: float32 [1536, 9, 128, 128], P(('row', 'col'))
Inputs may be any that keep to these rules, and one draw needn't show every extreme that they name: `density`: blocks on the main block diagonal are one half times the identity plus small entries; other blocks are small.
All inputs are finite; a program needn't handle non-finite values. No bound on the sum of `band_mask` on one device may be relied on, other than what follows from the above.
Results may differ from a plain program's by a relative error of at most 0.0003.
Values sent between devices are 32-bit elements; how exact they have to be, the bound alone decides.
A program may use at most 32 MiB of HBM per device.

v0:
```python
import jax
import jax.numpy as jnp
from jax import lax
from jax.sharding import PartitionSpec as P


def passed_along(value, axis, steps):
    count = lax.axis_size(axis)
    pairs = [(source, (source + steps) % count) for source in range(count)]
    return lax.ppermute(value, axis, pairs)


def band_product(left_rows, right_pad):
    row_count = left_rows.shape[0]
    diagonals = left_rows.shape[1]
    half_width = (diagonals - 1) // 2
    sums = [None] * diagonals
    for offset in range(diagonals):
        lowest = max(0, half_width - offset)
        highest = min(2 * half_width, 3 * half_width - offset)
        number = highest - lowest + 1
        start = lowest + offset - half_width
        right_rows = right_pad[offset : offset + row_count, lowest : highest + 1]
        product = jnp.einsum(
            "ixy,ifyz->ifxz", left_rows[:, offset], right_rows, precision=lax.Precision.HIGHEST
        )
        for place in range(number):
            target = start + place
            if sums[target] is None:
                sums[target] = product[:, place]
            else:
                sums[target] = sums[target] + product[:, place]
    return jnp.stack(sums, axis=1)


def local(density, band_mask):
    mask_float = band_mask.astype(jnp.float32)[:, :, None, None]
    masked = density * mask_float
    row_count = density.shape[0]
    diagonals = density.shape[1]
    half_width = (diagonals - 1) // 2
    reach = (half_width + row_count - 1) // row_count
    moved = {}
    for distance in list(range(reach, 0, -1)) + list(range(-1, -reach - 1, -1)):
        moved[distance] = passed_along(masked, ("row", "col"), distance)
    before_all = jnp.concatenate([moved[distance] for distance in range(reach, 0, -1)], axis=0)
    after_all = jnp.concatenate([moved[-distance] for distance in range(1, reach + 1)], axis=0)
    padded = jnp.concatenate([before_all, masked, after_all], axis=0)
    square = band_product(masked, padded)
    cube = band_product(square, padded)
    return (3.0 * square - 2.0 * cube) * mask_float


def solution(mesh):
    return jax.shard_map(
        local,
        mesh=mesh,
        in_specs=(P(("row", "col"), None, None, None), P(("row", "col"), None)),
        out_specs=P(("row", "col"), None, None, None),
        check_vma=False,
    )
```

profile of v0, /device:TPU:735, one launch (start us, length us, event | category | flops | bytes accessed | tf_op | source)
XLA Modules:
  0.0 72.9 jit_solution(6173378157707573600)
XLA Ops:
  0.0 0.7 convert_element_type.3
  0.7 0.1 copy.3
  0.8 1.4 %copy_multiply_fusion = f32[2,9,128,128]{3,2,0,1:T(8,128)S(1)} fusion(f32[2,9,128,128]{3,2,1,0:T(8,128)} %param.2, f32[2,9]{0,1:T(8,128)S(1)} %copy.3), kind=kLoop, calls=%fused_computation.24 | loop fusion | flops 294912 | bytes 2359368 | tf_op jit(solution)/shard_map/mul | solution.py:38
  2.2 4.3 %collective-permute-start = (f32[2,9,128,128]{3,2,0,1:T(8,128)S(1)}, f32[2,9,128,128]{3,2,0,1:T(8,128)S(1)}, u32[]{:S(2)}, u32[]{:S(2)}) collective-permute-start(f32[2,9,128,128]{3,2,0,1:T(8,128)S(1)} %copy_multiply_fusion), channel_id=1, source_target_pairs={{0,2},{1,3},{2,4},{3,5},{4,6},{5,7},{6,8},{7,9},{8,10},{9,11},{10,... | collective-permute-start | bytes 3538952 | tf_op jit(solution)/shard_map/ppermute | solution.py:10
  6.5 4.0 %collective-permute-start.1 = (f32[2,9,128,128]{3,2,0,1:T(8,128)S(1)}, f32[2,9,128,128]{3,2,0,1:T(8,128)S(1)}, u32[]{:S(2)}, u32[]{:S(2)}) collective-permute-start(f32[2,9,128,128]{3,2,0,1:T(8,128)S(1)} %copy_multiply_fusion), channel_id=1, source_target_pairs={{0,1},{1,2},{2,3},{3,4},{4,5},{5,6},{6,7},{7,8},{8,9},{9,10},{10,1... | collective-permute-start | bytes 3538952 | tf_op jit(solution)/shard_map/ppermute | solution.py:10
  10.5 2.2 %collective-permute-start.3 = (f32[2,9,128,128]{3,2,0,1:T(8,128)S(1)}, f32[2,9,128,128]{3,2,0,1:T(8,128)S(1)}, u32[]{:S(2)}, u32[]{:S(2)}) collective-permute-start(f32[2,9,128,128]{3,2,0,1:T(8,128)S(1)} %copy_multiply_fusion), channel_id=1, source_target_pairs={{0,766},{1,767},{2,0},{3,1},{4,2},{5,3},{6,4},{7,5},{8,6},{9,7},{1... | collective-permute-start | bytes 3538952 | tf_op jit(solution)/shard_map/ppermute | solution.py:10
  12.6 1.9 %collective-permute-start.2 = (f32[2,9,128,128]{3,2,0,1:T(8,128)S(1)}, f32[2,9,128,128]{3,2,0,1:T(8,128)S(1)}, u32[]{:S(2)}, u32[]{:S(2)}) collective-permute-start(f32[2,9,128,128]{3,2,0,1:T(8,128)S(1)} %copy_multiply_fusion), channel_id=1, source_target_pairs={{0,767},{1,0},{2,1},{3,2},{4,3},{5,4},{6,5},{7,6},{8,7},{9,8},{10,... | collective-permute-start | bytes 3538952 | tf_op jit(solution)/shard_map/ppermute | solution.py:10
  14.6 1.1 %convolution_bitcast_fusion.1 = f32[2,9,128,128]{3,2,0,1:T(8,128)S(1)} fusion(f32[2,9,128,128]{3,2,0,1:T(8,128)S(1)} %copy_multiply_fusion), kind=kOutput, calls=%fused_computation.7 | convolution fusion | flops 452984832 | bytes 2490368 | tf_op jit(solution)/shard_map/ixy,ifyz->ifxz/dot_general | solution.py:24
  15.7 15.4 %collective-permute-done = f32[2,9,128,128]{3,2,0,1:T(8,128)S(1)} collective-permute-done((f32[2,9,128,128]{3,2,0,1:T(8,128)S(1)}, f32[2,9,128,128]{3,2,0,1:T(8,128)S(1)}, u32[]{:S(2)}, u32[]{:S(2)}) %collective-permute-start) | collective-permute-done | bytes 1179680 | tf_op jit(solution)/shard_map/ppermute | solution.py:10
  31.1 0.1 constant_dynamic-update-slice_fusion.1
  31.2 13.7 %collective-permute-done.1 = f32[2,9,128,128]{3,2,0,1:T(8,128)S(1)} collective-permute-done((f32[2,9,128,128]{3,2,0,1:T(8,128)S(1)}, f32[2,9,128,128]{3,2,0,1:T(8,128)S(1)}, u32[]{:S(2)}, u32[]{:S(2)}) %collective-permute-start.1) | collective-permute-done | bytes 1179680 | tf_op jit(solution)/shard_map/ppermute | solution.py:10
  44.9 0.1 constant_dynamic-update-slice_fusion
  45.0 1.1 %fusion.5 = f32[2,8,128,128]{3,2,0,1:T(8,128)S(1)} fusion(f32[2,9,128,128]{3,2,0,1:T(8,128)S(1)} %copy_multiply_fusion, f32[2,9,128,128]{3,2,0,1:T(8,128)S(1)} %collective-permute-done.1), kind=kOutput, calls=%fused_computation.9 | convolution fusion | flops 403243008 | bytes 3538944 | tf_op jit(solution)/shard_map/ixy,ifyz->ifxz/dot_general | solution.py:24
  46.1 0.7 convolution_bitcast_fusion.13
  46.8 1.0 %convolution_bitcast_fusion.5 = f32[2,7,128,128]{3,2,0,1:T(8,128)S(1)} fusion(f32[2,9,128,128]{3,2,0,1:T(8,128)S(1)} %collective-permute-done.1, f32[2,9,128,128]{3,2,0,1:T(8,128)S(1)} %copy_multiply_fusion), kind=kOutput, calls=%fused_computation.15 | convolution fusion | flops 352321536 | bytes 2228224 | tf_op jit(solution)/shard_map/ixy,ifyz->ifxz/dot_general | solution.py:24
  47.8 0.9 %convolution_bitcast_fusion.9 = f32[2,6,128,128]{3,2,0,1:T(8,128)S(1)} fusion(f32[4,9,128,128]{3,2,0,1:T(8,128)S(1)} %constant_dynamic-update-slice_fusion, f32[2,9,128,128]{3,2,0,1:T(8,128)S(1)} %copy_multiply_fusion), kind=kOutput, calls=%fused_computation.19 | convolution fusion | flops 301989888 | bytes 3276800 | tf_op jit(solution)/shard_map/ixy,ifyz->ifxz/dot_general | solution.py:24
  48.6 9.5 %collective-permute-done.2 = f32[2,9,128,128]{3,2,0,1:T(8,128)S(1)} collective-permute-done((f32[2,9,128,128]{3,2,0,1:T(8,128)S(1)}, f32[2,9,128,128]{3,2,0,1:T(8,128)S(1)}, u32[]{:S(2)}, u32[]{:S(2)}) %collective-permute-start.2) | collective-permute-done | bytes 1179680 | tf_op jit(solution)/shard_map/ppermute | solution.py:10
  58.1 0.1 constant_dynamic-update-slice_fusion.3
  58.2 1.1 %fusion.7 = f32[2,8,128,128]{3,2,0,1:T(8,128)S(1)} fusion(f32[2,9,128,128]{3,2,0,1:T(8,128)S(1)} %collective-permute-done.2, f32[2,9,128,128]{3,2,0,1:T(8,128)S(1)} %copy_multiply_fusion), kind=kOutput, calls=%fused_computation.11 | convolution fusion | flops 403243008 | bytes 3538944 | tf_op jit(solution)/shard_map/ixy,ifyz->ifxz/dot_general | solution.py:24
  59.4 0.8 %convolution_bitcast_fusion.7 = f32[2,6,128,128]{3,2,0,1:T(8,128)S(1)} fusion(f32[4,9,128,128]{3,2,0,1:T(8,128)S(1)} %constant_dynamic-update-slice_fusion, f32[2,1,128,128]{3,2,0,1:T(8,128)S(1)} %get-tuple-element.20), kind=kOutput, calls=%fused_computation.17 | convolution fusion | flops 301989888 | bytes 3276800 | tf_op jit(solution)/shard_map/ixy,ifyz->ifxz/dot_general | solution.py:24
  60.2 0.0 collective-permute-done.3
  60.3 0.1 constant_dynamic-update-slice_fusion.2
  60.4 0.8 %convolution_bitcast_fusion.8 = f32[2,6,128,128]{3,2,0,1:T(8,128)S(1)} fusion(f32[4,9,128,128]{3,2,0,1:T(8,128)S(1)} %constant_dynamic-update-slice_fusion.2, f32[2,9,128,128]{3,2,0,1:T(8,128)S(1)} %copy_multiply_fusion), kind=kOutput, calls=%fused_computation.18 | convolution fusion | flops 301989888 | bytes 3276800 | tf_op jit(solution)/shard_map/ixy,ifyz->ifxz/dot_general | solution.py:24
  61.2 0.9 %convolution_bitcast_fusion.4 = f32[2,7,128,128]{3,2,0,1:T(8,128)S(1)} fusion(f32[2,9,128,128]{3,2,0,1:T(8,128)S(1)} %collective-permute-done.2, f32[2,9,128,128]{3,2,0,1:T(8,128)S(1)} %copy_multiply_fusion), kind=kOutput, calls=%fused_computation.14 | convolution fusion | flops 352321536 | bytes 2228224 | tf_op jit(solution)/shard_map/ixy,ifyz->ifxz/dot_general | solution.py:24
  62.2 0.1 constant_dynamic-update-slice_fusion.10
  62.2 0.1 constant_dynamic-update-slice_fusion.9
  62.3 0.7 convolution_bitcast_fusion.12
  63.0 0.1 constant_dynamic-update-slice_fusion.8
  63.1 0.1 constant_dynamic-update-slice_fusion.7
  63.2 0.1 constant_dynamic-update-slice_fusion.6
  63.3 0.9 %convolution_bitcast_fusion.6 = f32[2,6,128,128]{3,2,0,1:T(8,128)S(1)} fusion(f32[4,9,128,128]{3,2,0,1:T(8,128)S(1)} %constant_dynamic-update-slice_fusion.2, f32[2,1,128,128]{3,2,0,1:T(8,128)S(1)} %get-tuple-element.8), kind=kOutput, calls=%fused_computation.16 | convolution fusion | flops 301989888 | bytes 3276800 | tf_op jit(solution)/shard_map/ixy,ifyz->ifxz/dot_general | solution.py:24
  64.2 1.3 %convolution_bitcast_fusion = f32[2,9,128,128]{3,2,0,1:T(8,128)S(1)} fusion(f32[2,9,128,128]{3,2,0,1:T(8,128)S(1)} %copy_multiply_fusion, f32[2,1,128,128]{3,2,0,1:T(8,128)S(1)} %get-tuple-element.14), kind=kOutput, calls=%fused_computation.6 | convolution fusion | flops 452984832 | bytes 2490368 | tf_op jit(solution)/shard_map/ixy,ifyz->ifxz/dot_general | solution.py:24
  65.5 0.7 convolution_bitcast_fusion.11
  66.3 0.9 %convolution_bitcast_fusion.3 = f32[2,7,128,128]{3,2,0,1:T(8,128)S(1)} fusion(f32[2,9,128,128]{3,2,0,1:T(8,128)S(1)} %collective-permute-done.1, f32[2,1,128,128]{3,2,0,1:T(8,128)S(1)} %get-tuple-element.18), kind=kOutput, calls=%fused_computation.13 | convolution fusion | flops 352321536 | bytes 2228224 | tf_op jit(solution)/shard_map/ixy,ifyz->ifxz/dot_general | solution.py:24
  67.2 1.1 %fusion.4 = f32[2,8,128,128]{3,2,0,1:T(8,128)S(1)} fusion(f32[2,9,128,128]{3,2,0,1:T(8,128)S(1)} %copy_multiply_fusion, f32[2,9,128,128]{3,2,0,1:T(8,128)S(1)} %collective-permute-done.1, f32[2,1,128,128]{3,2,0,1:T(8,128)S(1)} %get-tuple-element.16), kind=kOutput, calls=%fused_computation.8 | convolution fusion | flops 403243008 | bytes 3538944 | tf_op jit(solution)/shard_map/ixy,ifyz->ifxz/dot_general | solution.py:24
  68.4 1.1 %fusion.6 = f32[2,8,128,128]{3,2,0,1:T(8,128)S(1)} fusion(f32[2,9,128,128]{3,2,0,1:T(8,128)S(1)} %collective-permute-done.2, f32[2,9,128,128]{3,2,0,1:T(8,128)S(1)} %copy_multiply_fusion, f32[2,1,128,128]{3,2,0,1:T(8,128)S(1)} %get-tuple-element.12), kind=kOutput, calls=%fused_computation.10 | convolution fusion | flops 403243008 | bytes 3538944 | tf_op jit(solution)/shard_map/ixy,ifyz->ifxz/dot_general | solution.py:24
  69.5 0.9 %convolution_bitcast_fusion.2 = f32[2,7,128,128]{3,2,0,1:T(8,128)S(1)} fusion(f32[2,9,128,128]{3,2,0,1:T(8,128)S(1)} %collective-permute-done.2, f32[2,1,128,128]{3,2,0,1:T(8,128)S(1)} %get-tuple-element.10), kind=kOutput, calls=%fused_computation.12 | convolution fusion | flops 352321536 | bytes 2228224 | tf_op jit(solution)/shard_map/ixy,ifyz->ifxz/dot_general | solution.py:24
  70.5 0.1 fusion.13
  70.6 0.7 convolution_bitcast_fusion.10
  71.3 0.1 fusion.12
  71.4 0.1 fusion.11
  71.6 0.2 subtract_multiply_fusion
  71.8 1.1 %copy.41 = f32[2,9,128,128]{3,2,1,0:T(8,128)} copy(f32[2,9,128,128]{3,2,0,1:T(8,128)S(1)} %subtract_multiply_fusion) | data formatting | bytes 2359296 | tf_op jit(solution)/shard_map/mul | solution.py:51
  (10 shorter events, 0.4 us)
Async XLA Ops:
  2.2 28.9 %collective-permute-start = (f32[2,9,128,128]{3,2,0,1:T(8,128)S(1)}, f32[2,9,128,128]{3,2,0,1:T(8,128)S(1)}, u32[]{:S(2)}, u32[]{:S(2)}) collective-permute-start(f32[2,9,128,128]{3,2,0,1:T(8,128)S(1)} %copy_multiply_fusion), channel_id=1, source_target_pairs={{0,2},{1,3},{2,4},{3,5},{4,6},{5,7},{6,8},{7,9},{8,10},{9,11},{10,... | collective-permute-start | bytes 3538952 | tf_op jit(solution)/shard_map/ppermute | solution.py:10
  6.5 38.4 %collective-permute-start.1 = (f32[2,9,128,128]{3,2,0,1:T(8,128)S(1)}, f32[2,9,128,128]{3,2,0,1:T(8,128)S(1)}, u32[]{:S(2)}, u32[]{:S(2)}) collective-permute-start(f32[2,9,128,128]{3,2,0,1:T(8,128)S(1)} %copy_multiply_fusion), channel_id=1, source_target_pairs={{0,1},{1,2},{2,3},{3,4},{4,5},{5,6},{6,7},{7,8},{8,9},{9,10},{10,1... | collective-permute-start | bytes 3538952 | tf_op jit(solution)/shard_map/ppermute | solution.py:10
  10.5 49.8 %collective-permute-start.3 = (f32[2,9,128,128]{3,2,0,1:T(8,128)S(1)}, f32[2,9,128,128]{3,2,0,1:T(8,128)S(1)}, u32[]{:S(2)}, u32[]{:S(2)}) collective-permute-start(f32[2,9,128,128]{3,2,0,1:T(8,128)S(1)} %copy_multiply_fusion), channel_id=1, source_target_pairs={{0,766},{1,767},{2,0},{3,1},{4,2},{5,3},{6,4},{7,5},{8,6},{9,7},{1... | collective-permute-start | bytes 3538952 | tf_op jit(solution)/shard_map/ppermute | solution.py:10
  12.6 45.4 %collective-permute-start.2 = (f32[2,9,128,128]{3,2,0,1:T(8,128)S(1)}, f32[2,9,128,128]{3,2,0,1:T(8,128)S(1)}, u32[]{:S(2)}, u32[]{:S(2)}) collective-permute-start(f32[2,9,128,128]{3,2,0,1:T(8,128)S(1)} %copy_multiply_fusion), channel_id=1, source_target_pairs={{0,767},{1,0},{2,1},{3,2},{4,3},{5,4},{6,5},{7,6},{8,7},{9,8},{10,... | collective-permute-start | bytes 3538952 | tf_op jit(solution)/shard_map/ppermute | solution.py:10
where the time goes:
time: 73.1 us; the launch traced here: 72.9 us
  waiting for transfers between devices  38.5 us (53%)
  matrix products  16.9 us (23%)
  starting transfers between devices  12.3 us (17%)
  other arithmetic  3.14 us (4%)
  local copies, waits for them, and re-layouts  1.63 us (2%)
    ppermute x4, waiting for transfers between devices, passed_along(): return lax.ppermute(value, axis, pairs)  38.5 us
    dot_general x18, matrix products, band_product(): jnp.einsum('ixy,ifyz->ifxz', left_rows[:, offset], right_rows, precision=...  16.9 us
    ppermute x4, starting transfers between devices, passed_along(): return lax.ppermute(value, axis, pairs)  12.3 us
  transfers between devices with their start and end apart: 4, of which 3 were waited for; matrix products, arithmetic and copies ran while one was open for 10% of the time, Pallas kernels for 0%

commit v1 on v0

v1 whole, which is shorter than its diff:
```python
import functools

import jax
import jax.numpy as jnp
from jax import lax
from jax.experimental import pallas as pl
from jax.experimental.pallas import tpu as pltpu
from jax.sharding import PartitionSpec as P

MESH = pl.DeviceIdType.MESH
F32, BF16 = jnp.float32, jnp.bfloat16
BLK = 128
K = 9
SLOTS = 2 * K
TILE = 2 * BLK

NEAR_SLOW = ((0, 4, 5), (1, 3, 6)), ((0, 2, 2), (1, 1, 2))
NEAR_FAST = ((0, 0, 6), (1, 0, 5)), ((0, 6, 2), (1, 5, 2))
FAR_SLOW = ((0, 8, 1), (1, 7, 2)), ((0, 6, 2), (1, 5, 2)), ((0, 4, 2), (1, 3, 2))
FAR_FAST = (((0, 0, 6), (1, 0, 5)),)


def kernel(rows, cols, x_ref, mask_ref, out_ref, held, marks, high, low, s_high, s_low, square, cube, send, recv, local_sem):
    core = lax.rem(lax.axis_index("col"), 2)
    g = lax.axis_index("row") * cols + lax.axis_index("col")

    def device(index):
        index = lax.rem(index + rows * cols, rows * cols)
        return lax.div(index, cols), lax.rem(index, cols)

    slow, fast = device(g + 2 * core - 1), device(g + 1 - 2 * core)

    barrier = pltpu.get_barrier_semaphore()
    for other in (slow, fast):
        pl.semaphore_signal(barrier, inc=1, device_id=other, device_id_type=MESH)

    own = pltpu.make_async_copy(x_ref, held.at[2], local_sem)
    own.start()
    for s in range(SLOTS):
        value = mask_ref[s // K, s % K].astype(F32)
        marks[2, s : s + 1, :] = jnp.full((1, BLK), value, F32)

    def entry(row, d):
        s = row * K + d
        return jnp.where(core == 0, s, SLOTS - 1 - s)

    def span(piece):
        row, d, count = piece
        s = row * K + d
        return pl.ds(jnp.where(core == 0, s, SLOTS - s - count), count)

    def corner(row, d):
        e = d + row
        r, c = jnp.where(core == 0, row, 1 - row), jnp.where(core == 0, e % 2, 1 - e % 2)
        return (
            e // 2 - 2,
            pl.ds(pl.multiple_of(r * BLK, BLK), BLK),
            pl.ds(pl.multiple_of(c * BLK, BLK), BLK),
        )

    for j in range(3):
        for row, d, k in ((0, K, j + 2), (1, -1, j)):
            _, r, c = corner(row, d)
            at = j if row == 0 else j + 2
            high[at, k, r, c] = jnp.zeros((BLK, BLK), BF16)
            low[at, k, r, c] = jnp.zeros((BLK, BLK), BF16)

    pl.semaphore_wait(barrier, 2)

    started = []

    def start(source, target, number, to):
        copy = pltpu.make_async_remote_copy(
            src_ref=source,
            dst_ref=target,
            send_sem=send.at[number],
            recv_sem=recv.at[number],
            device_id=to,
            device_id_type=MESH,
        )
        copy.start()
        started.append(copy)

    def landed(target, number):
        pltpu.make_async_remote_copy(
            src_ref=target,
            dst_ref=target,
            send_sem=send.at[number],
            recv_sem=recv.at[number],
            device_id=slow,
            device_id_type=MESH,
        ).wait_recv()

    def mirrored(piece):
        row, d, count = piece
        return 1 - row, K - d - count, count

    def give(source, at, pieces, number, to):
        for i, piece in enumerate(pieces):
            part = span(mirrored(piece))
            start(source.at[part], held.at[at, part], number + i, to)

    def take(at, pieces, number):
        for i, piece in enumerate(pieces):
            landed(held.at[at, span(piece)], number + i)

    start(marks.at[2], marks.at[1], 0, slow)
    start(marks.at[2], marks.at[3], 5, fast)
    give(x_ref, 1, NEAR_SLOW[0], 1, slow)
    give(x_ref, 3, NEAR_FAST[0], 6, fast)
    give(x_ref, 1, NEAR_SLOW[1], 3, slow)
    give(x_ref, 3, NEAR_FAST[1], 8, fast)

    def split(at, pieces):
        for row, first, count in pieces:
            def one(d, carry, row=row):
                s = entry(row, d)
                k, r, c = corner(row, d)
                value = held[at, s] * marks[at, pl.ds(s, 1), :]
                top = value.astype(BF16)
                high[at, at + k, r, c] = top
                low[at, at + k, r, c] = (value - top.astype(F32)).astype(BF16)
                return carry

            lax.fori_loop(first, first + count, one, 0)

    def product(a_high, a_low, j, k):
        b_high, b_low = high[j, k], low[j, k]
        dot = functools.partial(jnp.dot, preferred_element_type=F32)
        return dot(a_high, b_high) + (dot(a_high, b_low) + dot(a_low, b_high))

    def square_row(j, first, last, fresh=False):
        def one(k, carry):
            term = product(high[2, j], low[2, j], j, k)
            square[k] = term if fresh else square[k] + term
            return carry

        lax.fori_loop(first, last + 1, one, 0, unroll=True)

    def cube_row(j, first, last):
        def one(k, carry):
            cube[k] = cube[k] + product(s_high[j], s_low[j], j, k)
            return carry

        lax.fori_loop(first, last + 1, one, 0, unroll=True)

    def finish_square(j):
        if j in (0, 4):
            _, r, c = corner(*((1, -1) if j == 0 else (0, K)))
            square[j, r, c] = jnp.zeros((BLK, BLK), F32)
        value = square[j]
        top = value.astype(BF16)
        s_high[j] = top
        s_low[j] = (value - top.astype(F32)).astype(BF16)

    own.wait()
    split(2, ((0, 0, K), (1, 0, K)))
    cube[...] = jnp.zeros_like(cube)
    square_row(2, 0, 4, fresh=True)

    landed(marks.at[3], 5)
    start(marks.at[3], marks.at[0], 10, slow)
    take(3, NEAR_FAST[0], 6)
    for i, pieces in enumerate(FAR_SLOW):
        give(held.at[3], 0, pieces, 11 + 2 * i, slow)
    take(3, NEAR_FAST[1], 8)
    split(3, ((0, 0, 8), (1, 0, 7)))
    square_row(3, 1, 4)

    landed(marks.at[1], 0)
    start(marks.at[1], marks.at[4], 17, fast)
    take(1, NEAR_SLOW[0], 1)
    give(held.at[1], 4, FAR_FAST[0], 18, fast)
    split(1, NEAR_SLOW[0])
    square_row(1, 1, 3)
    take(1, NEAR_SLOW[1], 3)
    split(1, NEAR_SLOW[1])
    square_row(1, 0, 0)

    landed(marks.at[4], 17)
    take(4, FAR_FAST[0], 18)
    split(4, FAR_FAST[0])
    square_row(4, 2, 4)
    finish_square(4)
    cube_row(4, 2, 4)
    finish_square(3)
    cube_row(3, 1, 4)

    landed(marks.at[0], 10)
    for i, pieces in enumerate(FAR_SLOW):
        take(0, pieces, 11 + 2 * i)
        split(0, pieces)
        k = 2 - i
        square_row(0, k, k)
        finish_square(k)
        cube_row(k, 0, k + 2)

    for row in range(2):
        def one(d, carry, row=row):
            s = entry(row, d)
            k, r, c = corner(row, d)
            value = 3.0 * square[k + 2, r, c] - 2.0 * cube[k + 2, r, c]
            out_ref[s] = value * marks[2, pl.ds(s, 1), :]
            return carry

        lax.fori_loop(0, K, one, 0)

    for copy in started:
        copy.wait_send()


def solution(mesh):
    rows, cols = mesh.shape["row"], mesh.shape["col"]

    def local(density, band_mask):
        result = pl.pallas_call(
            functools.partial(kernel, rows, cols),
            out_shape=jax.ShapeDtypeStruct((SLOTS, BLK, BLK), F32),
            in_specs=[
                pl.BlockSpec(memory_space=pltpu.HBM),
                pl.BlockSpec(memory_space=pltpu.SMEM),
            ],
            out_specs=pl.BlockSpec(memory_space=pltpu.VMEM),
            scratch_shapes=[
                pltpu.VMEM((5, SLOTS, BLK, BLK), F32),
                pltpu.VMEM((5, 24, BLK), F32),
                pltpu.VMEM((5, 5, TILE, TILE), BF16),
                pltpu.VMEM((5, 5, TILE, TILE), BF16),
                pltpu.VMEM((5, TILE, TILE), BF16),
                pltpu.VMEM((5, TILE, TILE), BF16),
                pltpu.VMEM((5, TILE, TILE), F32),
                pltpu.VMEM((5, TILE, TILE), F32),
                pltpu.SemaphoreType.DMA((20,)),
                pltpu.SemaphoreType.DMA((20,)),
                pltpu.SemaphoreType.DMA,
            ],
            compiler_params=pltpu.CompilerParams(
                collective_id=0, has_side_effects=True, vmem_limit_bytes=40 << 20
            ),
        )(pltpu.with_memory_space_constraint(density.reshape(SLOTS, BLK, BLK), pltpu.HBM), band_mask)
        return result.reshape(density.shape)

    return jax.shard_map(
        local,
        mesh=mesh,
        in_specs=(P(("row", "col"), None, None, None), P(("row", "col"), None)),
        out_specs=P(("row", "col"), None, None, None),
        check_vma=False,
    )
```

time: 73.1 us -> 39.1 us (0.53)
  the two profiles are of different devices: /device:TPU:735 before, /device:TPU:1 now
where the time goes in v1:
time: 39.1 us; the launch traced here: 39 us
  Pallas kernels  37.3 us (95%)
  local copies, waits for them, and re-layouts  1.69 us (4%)
    pallas_call x1, Pallas kernels, local(): pl.pallas_call(functools.partial(kernel, rows, cols), out_shape=jax.Shape...  37.3 us
    unnamed x3, local copies, waits for them, and re-layouts  1.69 us

profile of v1, /device:TPU:1, one launch (start us, length us, event | category | flops | bytes accessed | tf_op | source)
XLA Modules:
  0.0 39.0 jit_solution(10055352998704827366)
XLA Ops:
  0.0 0.0 copy-start
  0.0 0.7 %copy-done = s32[2,9]{1,0:T(2,128)S(1)} copy-done((s32[2,9]{1,0:T(2,128)S(1)}, s32[2,9]{1,0:T(2,128)}, u32[]{:S(2)}) %copy-start) | copy-done | bytes 96
  0.7 37.3 %shard_map.28 = f32[18,128,128]{2,1,0:T(8,128)S(1)} custom-call(f32[18,128,128]{2,1,0:T(8,128)} %bitcast.3, s32[2,9]{1,0:T(2,128)S(1)} %copy-done), custom_call_target="tpu_custom_call" | custom-call | tf_op jit(solution)/shard_map/pallas_call | solution.py:216
  38.0 1.0 %copy.4 = f32[2,9,128,128]{3,2,1,0:T(8,128)} copy(f32[2,9,128,128]{3,2,1,0:T(8,128)S(1)} %bitcast.2) | data formatting | bytes 2359296
Async XLA Ops:
  0.0 0.7 %copy-start = (s32[2,9]{1,0:T(2,128)S(1)}, s32[2,9]{1,0:T(2,128)}, u32[]{:S(2)}) copy-start(s32[2,9]{1,0:T(2,128)} %mask_ref.1) | copy-start | bytes 220

commit v2 on v1

v2 whole, which is shorter than its diff:
```python
import functools

import jax
import jax.numpy as jnp
from jax import lax
from jax.experimental import pallas as pl
from jax.experimental.pallas import tpu as pltpu
from jax.sharding import PartitionSpec as P

MESH = pl.DeviceIdType.MESH
F32, BF16 = jnp.float32, jnp.bfloat16
BLK = 128
K = 9
SLOTS = 2 * K
TILE = 2 * BLK

NEAR_SLOW = (
    ((0, 8, 1), (1, 7, 2)),
    ((0, 6, 2), (1, 5, 2)),
    ((0, 4, 2), (1, 3, 2)),
    ((0, 2, 2), (1, 1, 2)),
)
NEAR_FAST = ((0, 0, 6), (1, 0, 5)), ((0, 6, 2), (1, 5, 2))
FAR = ((0, 8, 1), (1, 7, 2)), ((0, 6, 2), (1, 5, 2)), ((0, 5, 1), (1, 4, 1)), ((0, 4, 1), (1, 3, 1))

MARKS_SLOW, MARKS_FAST, MARKS_FAR = 0, 1, 2
AT_SLOW, AT_FAST, AT_FAR, SEMAPHORES = 4, 12, 16, 32


def kernel(rows, cols, x_ref, mask_ref, out_ref, held, masks, marks, high, low, s_high, s_low, square, cube, send, recv, local_sem, ready):
    core = lax.rem(lax.axis_index("col"), 2)
    g = lax.axis_index("row") * cols + lax.axis_index("col")

    def device(index):
        index = lax.rem(index + rows * cols, rows * cols)
        return lax.div(index, cols), lax.rem(index, cols)

    slow, fast = device(g + 2 * core - 1), device(g + 1 - 2 * core)

    barrier = pltpu.get_barrier_semaphore()
    pl.semaphore_signal(barrier, inc=1, device_id=slow, device_id_type=MESH)

    @pl.when(core == 1)
    def _():
        pl.semaphore_signal(barrier, inc=1, device_id=fast, device_id_type=MESH)

    own = pltpu.make_async_copy(x_ref, held.at[2], local_sem.at[0])
    own_mask = pltpu.make_async_copy(mask_ref, masks.at[2], local_sem.at[1])
    own.start()
    own_mask.start()

    def entry(flip, row, d):
        s = row * K + d
        return jnp.where(flip == 0, s, SLOTS - 1 - s)

    def span(flip, piece):
        row, d, count = piece
        s = row * K + d
        return pl.ds(jnp.where(flip == 0, s, SLOTS - s - count), count)

    def half(flip, r):
        return pl.ds(pl.multiple_of(jnp.where(flip == 0, r, 1 - r) * BLK, BLK), BLK)

    def place(flip, row, d):
        e = d + row
        return e // 2 - 2, half(flip, row), half(flip, e % 2)

    started = []

    def start(source, target, number, to):
        copy = pltpu.make_async_remote_copy(
            src_ref=source,
            dst_ref=target,
            send_sem=send.at[number],
            recv_sem=recv.at[number],
            device_id=to,
            device_id_type=MESH,
        )
        copy.start()
        started.append(copy)

    def landed(target, number):
        pltpu.make_async_remote_copy(
            src_ref=target,
            dst_ref=target,
            send_sem=send.at[number],
            recv_sem=recv.at[number],
            device_id=slow,
            device_id_type=MESH,
        ).wait_recv()

    def give(source, at, flip, pieces, number, to):
        for i, piece in enumerate(pieces):
            part = span(flip, piece)
            start(source.at[part], held.at[at, part], number + i, to)

    def take(at, flip, pieces, number):
        for i, piece in enumerate(pieces):
            landed(held.at[at, span(flip, piece)], number + i)

    pl.semaphore_wait(barrier, 2 - core)

    @pl.when(core == 0)
    def _():
        pl.semaphore_signal(ready, inc=1, device_id=fast, device_id_type=MESH)

    start(mask_ref, masks.at[1], MARKS_SLOW, slow)
    for i, pieces in enumerate(NEAR_SLOW):
        give(x_ref, 1, 1 - core, pieces, AT_SLOW + 2 * i, slow)

    for j in range(3):
        for row, d, at, k in ((0, K, j, j + 2), (1, -1, j + 2, j)):
            _, r, c = place(core, row, d)
            high[at, k, r, c] = jnp.zeros((BLK, BLK), BF16)
            low[at, k, r, c] = jnp.zeros((BLK, BLK), BF16)
    cube[...] = jnp.zeros_like(cube)

    def mark(at):
        value = masks[at].astype(F32)
        for s in range(SLOTS):
            one = value[s // K : s // K + 1, s % K : s % K + 1]
            marks[at, s : s + 1, :] = jnp.broadcast_to(one, (1, BLK))

    def split(at, flip, pieces, turned=None):
        for row, first, count in pieces:
            def one(d, carry, row=row):
                s = entry(flip, row, d)
                k, r, c = place(flip, row, d)
                value = held[at, s] * marks[at, pl.ds(s, 1), :]
                top = value.astype(BF16)
                k = at + k if turned is None else turned(k)
                high[at, k, r, c] = top
                low[at, k, r, c] = (value - top.astype(F32)).astype(BF16)
                return carry

            lax.fori_loop(first, first + count, one, 0)

    dot = functools.partial(jnp.dot, preferred_element_type=F32)

    def product(a_high, a_low, b_high, b_low):
        return dot(a_high, b_high) + (dot(a_high, b_low) + dot(a_low, b_high))

    def square_row(j, tiles, fresh=False):
        for k in tiles:
            term = product(high[2, j], low[2, j], high[j, k], low[j, k])
            square[k] = term if fresh else square[k] + term

    def cube_row(j, tiles):
        for k in tiles:
            cube[k] = cube[k] + product(s_high[j], s_low[j], high[j, k], low[j, k])

    def finish_square(j, r=slice(None), c=slice(None)):
        value = square[j, r, c]
        top = value.astype(BF16)
        s_high[j, r, c] = top
        s_low[j, r, c] = (value - top.astype(F32)).astype(BF16)

    def give_out(flip, pieces, tile):
        for row, first, count in pieces:
            def one(d, carry, row=row):
                s = entry(flip, row, d)
                k, r, c = place(flip, row, d)
                k = tile(k + 2)
                value = 3.0 * square[k, r, c] - 2.0 * cube[k, r, c]
                out_ref[s] = value * marks[2, pl.ds(s, 1), :]
                return carry

            lax.fori_loop(first, first + count, one, 0)

    own.wait()
    own_mask.wait()
    mark(2)
    split(2, core, ((0, 0, K), (1, 0, K)))

    @pl.when(core == 1)
    def _():
        pl.semaphore_wait(ready, 1)

    start(mask_ref, masks.at[3], MARKS_FAST, fast)
    for i, pieces in enumerate(NEAR_FAST):
        give(x_ref, 3, 1 - core, pieces, AT_FAST + 2 * i, fast)
    square_row(2, range(5), fresh=True)

    landed(masks.at[3], MARKS_FAST)
    start(masks.at[3], masks.at[0], MARKS_FAR, slow)
    take(3, core, NEAR_FAST[0], AT_FAST)
    for i, pieces in enumerate(FAR):
        give(held.at[3], 0, 1 - core, pieces, AT_FAR + 2 * i, slow)
    take(3, core, NEAR_FAST[1], AT_FAST + 2)
    mark(3)
    split(3, core, ((0, 0, 8), (1, 0, 7)))
    square_row(3, (1, 2, 3, 4))

    landed(masks.at[1], MARKS_SLOW)
    start(masks.at[1], masks.at[4], MARKS_FAR + 1, fast)
    mark(1)
    for i, pieces in enumerate(NEAR_SLOW):
        take(1, core, pieces, AT_SLOW + 2 * i)
        if i < 2:
            give(held.at[1], 4, core, pieces, AT_FAR + 8 + 2 * i, fast)
        elif i == 2:
            for n, part in enumerate(FAR[2:]):
                give(held.at[1], 4, core, part, AT_FAR + 12 + 2 * n, fast)
        split(1, core, pieces)
        square_row(1, (3 - i,))

    for last in (False, True):
        side = jnp.where((g == 1) == last, 1, 0)
        flip = jnp.where(side == 0, core, 1 - core)

        def tile(k, side=side):
            return jnp.where(side == 0, k, 4 - k)

        far = tile(0)
        number = AT_FAR + 8 * side
        landed(masks.at[far], MARKS_FAR + side)
        mark(far)
        for i, pieces in enumerate(FAR):
            take(far, flip, pieces, number + 2 * i)
            split(far, flip, pieces, turned=lambda k: tile(k))
            if i == 0:
                square_row(far, (2,))
                if last:
                    finish_square(2)
                    cube_row(2, range(5))
            elif i == 1:
                square_row(far, (tile(1),))
                finish_square(tile(1))
                cube_row(tile(1), [tile(k) for k in range(4)])
            elif i == 2:
                r0, r1 = half(flip, 0), half(flip, 1)
                c0, c1 = r0, r1
                everything = slice(None)
                square[far, :, c1] += product(high[2, far], low[2, far], high[far, far, :, c1], low[far, far, :, c1])
                finish_square(far, everything, c1)
                a_high, a_low = s_high[far, :, c1], s_low[far, :, c1]
                for k in (tile(1), tile(2)):
                    cube[k] += product(a_high, a_low, high[far, k, c1, :], low[far, k, c1, :])
                cube[far, :, c1] += product(a_high, a_low, high[far, far, c1, c1], low[far, far, c1, c1])
                if last:
                    give_out(flip, ((0, 5, 4), (1, 0, K)), tile)
            else:
                square[far, r0, c0] += product(high[2, far, r0, :], low[2, far, r0, :], high[far, far, :, c0], low[far, far, :, c0])
                finish_square(far, r0, c0)
                a_high, a_low = s_high[far, r0, c0], s_low[far, r0, c0]
                cube[far, r0, c0] += product(s_high[far, r0, :], s_low[far, r0, :], high[far, far, :, c0], low[far, far, :, c0])
                cube[far, r0, c1] += product(a_high, a_low, high[far, far, c0, c1], low[far, far, c0, c1])
                k = tile(1)
                cube[k, r0, :] += product(a_high, a_low, high[far, k, c0, :], low[far, k, c0, :])
                cube[2, r0, c0] += product(a_high, a_low, high[far, 2, c0, c0], low[far, 2, c0, c0])
                if last:
                    give_out(flip, ((0, 0, 5),), tile)

    for copy in started:
        copy.wait_send()


def solution(mesh):
    rows, cols = mesh.shape["row"], mesh.shape["col"]

    def local(density, band_mask):
        blocks = pltpu.with_memory_space_constraint(
            density.reshape(SLOTS, BLK, BLK), pltpu.HBM
        )
        mask = pltpu.with_memory_space_constraint(band_mask, pltpu.HBM)
        result = pl.pallas_call(
            functools.partial(kernel, rows, cols),
            out_shape=jax.ShapeDtypeStruct((SLOTS, BLK, BLK), F32),
            in_specs=[
                pl.BlockSpec(memory_space=pltpu.HBM),
                pl.BlockSpec(memory_space=pltpu.HBM),
            ],
            out_specs=pl.BlockSpec(memory_space=pltpu.VMEM),
            scratch_shapes=[
                pltpu.VMEM((5, SLOTS, BLK, BLK), F32),
                pltpu.VMEM((5, 2, K), jnp.int32),
                pltpu.VMEM((5, 24, BLK), F32),
                pltpu.VMEM((5, 5, TILE, TILE), BF16),
                pltpu.VMEM((5, 5, TILE, TILE), BF16),
                pltpu.VMEM((5, TILE, TILE), BF16),
                pltpu.VMEM((5, TILE, TILE), BF16),
                pltpu.VMEM((5, TILE, TILE), F32),
                pltpu.VMEM((5, TILE, TILE), F32),
                pltpu.SemaphoreType.DMA((SEMAPHORES,)),
                pltpu.SemaphoreType.DMA((SEMAPHORES,)),
                pltpu.SemaphoreType.DMA((2,)),
                pltpu.SemaphoreType.REGULAR,
            ],
            compiler_params=pltpu.CompilerParams(
                collective_id=0, has_side_effects=True, vmem_limit_bytes=40 << 20
            ),
        )(blocks, mask)
        return result.reshape(density.shape)

    return jax.shard_map(
        local,
        mesh=mesh,
        in_specs=(P(("row", "col"), None, None, None), P(("row", "col"), None)),
        out_specs=P(("row", "col"), None, None, None),
        check_vma=False,
    )
```

time: 39.1 us -> 33.6 us (0.86)
  Pallas kernels: 37.3 us -> 32.4 us
  local copies, waits for them, and re-layouts: 1.69 us -> 1.02 us
    pallas_call x1, Pallas kernels: 37.3 us -> 32.4 us  [local(): pl.pallas_call(functools.partial(kernel, rows, cols), out_shape=jax.Shape...]
    unnamed x3 -> x1, local copies, waits for them, and re-layouts: 1.69 us -> 1.02 us
where the time goes in v2:
time: 33.6 us; the launch traced here: 33.4 us
  Pallas kernels  32.4 us (96%)
  local copies, waits for them, and re-layouts  1.02 us (3%)
    pallas_call x1, Pallas kernels, local(): pl.pallas_call(functools.partial(kernel, rows, cols), out_shape=jax.Shape...  32.4 us
    unnamed x1, local copies, waits for them, and re-layouts  1.02 us

profile of v2, /device:TPU:1, one launch (start us, length us, event | category | flops | bytes accessed | tf_op | source)
XLA Modules:
  0.0 33.4 jit_solution(6347095025617368024)
XLA Ops:
  0.0 32.4 %shard_map.28 = f32[18,128,128]{2,1,0:T(8,128)S(1)} custom-call(f32[18,128,128]{2,1,0:T(8,128)} %bitcast.3, s32[2,9]{1,0:T(2,128)} %mask_ref.1), custom_call_target="tpu_custom_call" | custom-call | tf_op jit(solution)/shard_map/pallas_call | solution.py:266
  32.4 1.0 %copy.4 = f32[2,9,128,128]{3,2,1,0:T(8,128)} copy(f32[2,9,128,128]{3,2,1,0:T(8,128)S(1)} %bitcast.2) | data formatting | bytes 2359296

commit v3 on v2

--- a/solution.py
+++ b/solution.py
@@ -14,20 +14,13 @@
 SLOTS = 2 * K
 TILE = 2 * BLK
 
-NEAR_SLOW = (
-    ((0, 8, 1), (1, 7, 2)),
-    ((0, 6, 2), (1, 5, 2)),
-    ((0, 4, 2), (1, 3, 2)),
-    ((0, 2, 2), (1, 1, 2)),
-)
-NEAR_FAST = ((0, 0, 6), (1, 0, 5)), ((0, 6, 2), (1, 5, 2))
 FAR = ((0, 8, 1), (1, 7, 2)), ((0, 6, 2), (1, 5, 2)), ((0, 5, 1), (1, 4, 1)), ((0, 4, 1), (1, 3, 1))
-
-MARKS_SLOW, MARKS_FAST, MARKS_FAR = 0, 1, 2
-AT_SLOW, AT_FAST, AT_FAR, SEMAPHORES = 4, 12, 16, 32
-
-
-def kernel(rows, cols, x_ref, mask_ref, out_ref, held, masks, marks, high, low, s_high, s_low, square, cube, send, recv, local_sem, ready):
+NEAR = (*FAR, ((0, 2, 2), (1, 1, 2)))
+
+PIECES = 10
+
+
+def kernel(rows, cols, x_ref, mask_ref, out_ref, held, masks, marks, high, low, s_high, s_low, square, cube, send, mask_sem, near_sem, far_sem, local_sem, ready):
     core = lax.rem(lax.axis_index("col"), 2)
     g = lax.axis_index("row") * cols + lax.axis_index("col")
 
@@ -37,8 +30,12 @@
 
     slow, fast = device(g + 2 * core - 1), device(g + 1 - 2 * core)
 
+    first, last_one = g == 0, g == rows * cols - 1
     barrier = pltpu.get_barrier_semaphore()
-    pl.semaphore_signal(barrier, inc=1, device_id=slow, device_id_type=MESH)
+
+    @pl.when(jnp.logical_not(last_one))
+    def _():
+        pl.semaphore_signal(barrier, inc=1, device_id=slow, device_id_type=MESH)
 
     @pl.when(core == 1)
     def _():
@@ -65,48 +62,76 @@
         e = d + row
         return e // 2 - 2, half(flip, row), half(flip, e % 2)
 
-    started = []
-
-    def start(source, target, number, to):
+    def start(source, target, receiving, sending, to):
         copy = pltpu.make_async_remote_copy(
             src_ref=source,
             dst_ref=target,
-            send_sem=send.at[number],
-            recv_sem=recv.at[number],
+            send_sem=send.at[sending],
+            recv_sem=receiving,
             device_id=to,
             device_id_type=MESH,
         )
         copy.start()
-        started.append(copy)
-
-    def landed(target, number):
+
+    def landed(target, receiving):
         pltpu.make_async_remote_copy(
             src_ref=target,
             dst_ref=target,
-            send_sem=send.at[number],
-            recv_sem=recv.at[number],
+            send_sem=send.at[0],
+            recv_sem=receiving,
             device_id=slow,
             device_id_type=MESH,
         ).wait_recv()
 
-    def give(source, at, flip, pieces, number, to):
+    def sent(source, sending):
+        pltpu.make_async_remote_copy(
+            src_ref=source,
+            dst_ref=source,
+            send_sem=send.at[sending],
+            recv_sem=near_sem.at[0],
+            device_id=slow,
+            device_id_type=MESH,
+        ).wait_send()
+
+    def give(source, at, flip, pieces, semaphores, number, sending, to):
         for i, piece in enumerate(pieces):
             part = span(flip, piece)
-            start(source.at[part], held.at[at, part], number + i, to)
-
-    def take(at, flip, pieces, number):
+            start(source.at[part], held.at[at, part], semaphores.at[number + i], sending, to)
+
+    def take(at, flip, pieces, semaphores, number):
         for i, piece in enumerate(pieces):
-            landed(held.at[at, span(flip, piece)], number + i)
-
-    pl.semaphore_wait(barrier, 2 - core)
+            landed(held.at[at, span(flip, piece)], semaphores.at[number + i])
+
+    def give_own(side, to):
+        at, flip = 1 + 2 * side, core if side else 1 - core
+        start(mask_ref, masks.at[at], mask_sem.at[side], side, to)
+        for i, pieces in enumerate(NEAR):
+            give(x_ref, at, flip, pieces, near_sem, PIECES * side + 2 * i, 2 + side, to)
+
+    pl.semaphore_wait(barrier, jnp.where(first, 1, 2 - core))
 
     @pl.when(core == 0)
     def _():
         pl.semaphore_signal(ready, inc=1, device_id=fast, device_id_type=MESH)
 
-    start(mask_ref, masks.at[1], MARKS_SLOW, slow)
-    for i, pieces in enumerate(NEAR_SLOW):
-        give(x_ref, 1, 1 - core, pieces, AT_SLOW + 2 * i, slow)
+    @pl.when(last_one)
+    def _():
+        pl.semaphore_signal(ready, inc=1, device_id=slow, device_id_type=MESH)
+
+    @pl.when(jnp.logical_not(first))
+    def _():
+        give_own(0, slow)
+
+    @pl.when(core == 1)
+    def _():
+        pl.semaphore_wait(ready, 1)
+
+    give_own(1, fast)
+
+    @pl.when(first)
+    def _():
+        pl.semaphore_wait(ready, 1)
+        give_own(0, slow)
 
     for j in range(3):
         for row, d, at, k in ((0, K, j, j + 2), (1, -1, j + 2, j)):
@@ -172,37 +197,23 @@
     mark(2)
     split(2, core, ((0, 0, K), (1, 0, K)))
 
-    @pl.when(core == 1)
-    def _():
-        pl.semaphore_wait(ready, 1)
-
-    start(mask_ref, masks.at[3], MARKS_FAST, fast)
-    for i, pieces in enumerate(NEAR_FAST):
-        give(x_ref, 3, 1 - core, pieces, AT_FAST + 2 * i, fast)
     square_row(2, range(5), fresh=True)
 
-    landed(masks.at[3], MARKS_FAST)
-    start(masks.at[3], masks.at[0], MARKS_FAR, slow)
-    take(3, core, NEAR_FAST[0], AT_FAST)
-    for i, pieces in enumerate(FAR):
-        give(held.at[3], 0, 1 - core, pieces, AT_FAR + 2 * i, slow)
-    take(3, core, NEAR_FAST[1], AT_FAST + 2)
-    mark(3)
-    split(3, core, ((0, 0, 8), (1, 0, 7)))
-    square_row(3, (1, 2, 3, 4))
-
-    landed(masks.at[1], MARKS_SLOW)
-    start(masks.at[1], masks.at[4], MARKS_FAR + 1, fast)
-    mark(1)
-    for i, pieces in enumerate(NEAR_SLOW):
-        take(1, core, pieces, AT_SLOW + 2 * i)
-        if i < 2:
-            give(held.at[1], 4, core, pieces, AT_FAR + 8 + 2 * i, fast)
-        elif i == 2:
-            for n, part in enumerate(FAR[2:]):
-                give(held.at[1], 4, core, part, AT_FAR + 12 + 2 * n, fast)
-        split(1, core, pieces)
-        square_row(1, (3 - i,))
+    for side in (1, 0):
+        at, far = (3, 0) if side else (1, 4)
+        flip = 1 - core if side else core
+        other = slow if side else fast
+        landed(masks.at[at], mask_sem.at[side])
+        start(masks.at[at], masks.at[far], mask_sem.at[3 - side], 4 + side, other)
+        mark(at)
+        for i, pieces in enumerate(NEAR):
+            take(at, flip, pieces, near_sem, PIECES * side + 2 * i)
+            if i < len(FAR):
+                give(held.at[at], far, flip, pieces, far_sem, PIECES * (1 - side) + 2 * i, 6 + side, other)
+            split(at, flip, pieces, turned=(lambda k: 3 - k) if side else None)
+            if i != 2:
+                k = (3, 2, 1, 1, 0)[i]
+                square_row(at, (4 - k if side else k,))
 
     for last in (False, True):
         side = jnp.where((g == 1) == last, 1, 0)
@@ -212,11 +223,10 @@
             return jnp.where(side == 0, k, 4 - k)
 
         far = tile(0)
-        number = AT_FAR + 8 * side
-        landed(masks.at[far], MARKS_FAR + side)
+        landed(masks.at[far], mask_sem.at[2 + side])
         mark(far)
         for i, pieces in enumerate(FAR):
-            take(far, flip, pieces, number + 2 * i)
+            take(far, flip, pieces, far_sem, PIECES * side + 2 * i)
             split(far, flip, pieces, turned=lambda k: tile(k))
             if i == 0:
                 square_row(far, (2,))
@@ -251,8 +261,11 @@
                 if last:
                     give_out(flip, ((0, 0, 5),), tile)
 
-    for copy in started:
-        copy.wait_send()
+    for n in range(2):
+        sent(masks.at[2], n)
+        sent(held.at[2, pl.ds(0, 15)], 2 + n)
+        sent(masks.at[2], 4 + n)
+        sent(held.at[2, pl.ds(0, 11)], 6 + n)
 
 
 def solution(mesh):
@@ -281,8 +294,10 @@
                 pltpu.VMEM((5, TILE, TILE), BF16),
                 pltpu.VMEM((5, TILE, TILE), F32),
                 pltpu.VMEM((5, TILE, TILE), F32),
-                pltpu.SemaphoreType.DMA((SEMAPHORES,)),
-                pltpu.SemaphoreType.DMA((SEMAPHORES,)),
+                pltpu.SemaphoreType.DMA((8,)),
+                pltpu.SemaphoreType.DMA((4,)),
+                pltpu.SemaphoreType.DMA((2 * PIECES,)),
+                pltpu.SemaphoreType.DMA((2 * PIECES,)),
                 pltpu.SemaphoreType.DMA((2,)),
                 pltpu.SemaphoreType.REGULAR,
             ],

time: 33.6 us -> 31.8 us (0.946)
  Pallas kernels: 32.4 us -> 30.7 us
    pallas_call x1, Pallas kernels: 32.4 us -> 30.7 us  [local(): pl.pallas_call(functools.partial(kernel, rows, cols), out_shape=jax.Shape...]
where the time goes in v3:
time: 31.8 us; the launch traced here: 31.7 us
  Pallas kernels  30.7 us (97%)
  local copies, waits for them, and re-layouts  1.02 us (3%)
    pallas_call x1, Pallas kernels, local(): pl.pallas_call(functools.partial(kernel, rows, cols), out_shape=jax.Shape...  30.7 us
    unnamed x1, local copies, waits for them, and re-layouts  1.02 us

profile of v3, /device:TPU:1, one launch (start us, length us, event | category | flops | bytes accessed | tf_op | source)
XLA Modules:
  0.0 31.7 jit_solution(214138680843530206)
XLA Ops:
  0.0 30.7 %shard_map.28 = f32[18,128,128]{2,1,0:T(8,128)S(1)} custom-call(f32[18,128,128]{2,1,0:T(8,128)} %bitcast.3, s32[2,9]{1,0:T(2,128)} %mask_ref.1), custom_call_target="tpu_custom_call" | custom-call | tf_op jit(solution)/shard_map/pallas_call | solution.py:279
  30.7 1.0 %copy.4 = f32[2,9,128,128]{3,2,1,0:T(8,128)} copy(f32[2,9,128,128]{3,2,1,0:T(8,128)S(1)} %bitcast.2) | data formatting | bytes 2359296

commit v4 on v3

--- a/solution.py
+++ b/solution.py
@@ -21,8 +21,8 @@
 
 
 def kernel(rows, cols, x_ref, mask_ref, out_ref, held, masks, marks, high, low, s_high, s_low, square, cube, send, mask_sem, near_sem, far_sem, local_sem, ready):
-    core = lax.rem(lax.axis_index("col"), 2)
-    g = lax.axis_index("row") * cols + lax.axis_index("col")
+    mine, col = lax.axis_index("row"), lax.axis_index("col")
+    core, g = lax.rem(col, 2), mine * cols + col
 
     def device(index):
         index = lax.rem(index + rows * cols, rows * cols)
@@ -30,16 +30,18 @@
 
     slow, fast = device(g + 2 * core - 1), device(g + 1 - 2 * core)
 
-    first, last_one = g == 0, g == rows * cols - 1
+    first, second, last = g == 0, g == 1, g == rows * cols - 1
     barrier = pltpu.get_barrier_semaphore()
 
-    @pl.when(jnp.logical_not(last_one))
-    def _():
-        pl.semaphore_signal(barrier, inc=1, device_id=slow, device_id_type=MESH)
-
-    @pl.when(core == 1)
-    def _():
-        pl.semaphore_signal(barrier, inc=1, device_id=fast, device_id_type=MESH)
+    def here(condition, *others):
+        @pl.when(condition)
+        def _():
+            for other in others:
+                pl.semaphore_signal(barrier, inc=1, device_id=other, device_id_type=MESH)
+
+    here(jnp.logical_not(last), slow)
+    here(core == 1, fast)
+    here(second, (rows - 1, cols - 1))
 
     own = pltpu.make_async_copy(x_ref, held.at[2], local_sem.at[0])
     own_mask = pltpu.make_async_copy(mask_ref, masks.at[2], local_sem.at[1])
@@ -102,36 +104,51 @@
         for i, piece in enumerate(pieces):
             landed(held.at[at, span(flip, piece)], semaphores.at[number + i])
 
-    def give_own(side, to):
-        at, flip = 1 + 2 * side, core if side else 1 - core
-        start(mask_ref, masks.at[at], mask_sem.at[side], side, to)
-        for i, pieces in enumerate(NEAR):
-            give(x_ref, at, flip, pieces, near_sem, PIECES * side + 2 * i, 2 + side, to)
-
-    pl.semaphore_wait(barrier, jnp.where(first, 1, 2 - core))
+    def give_mask(at, semaphore, side, to):
+        start(mask_ref, masks.at[at], mask_sem.at[semaphore], side, to)
+
+    pl.semaphore_wait(barrier, jnp.where(first, 1, jnp.where(last, 2, 2 - core)))
 
     @pl.when(core == 0)
     def _():
         pl.semaphore_signal(ready, inc=1, device_id=fast, device_id_type=MESH)
 
-    @pl.when(last_one)
+    @pl.when(last)
     def _():
         pl.semaphore_signal(ready, inc=1, device_id=slow, device_id_type=MESH)
 
-    @pl.when(jnp.logical_not(first))
-    def _():
-        give_own(0, slow)
+    def give_slow():
+        give_mask(1, 0, 0, slow)
+        for i, pieces in enumerate(FAR):
+            give(x_ref, 1, 1 - core, pieces, near_sem, 2 * i, 2, slow)
+        give_rest()
+
+    def give_rest():
+        give(x_ref, 1, 1 - core, NEAR[4], near_sem, 8, 2, slow)
+
+    @pl.when(jnp.logical_not(jnp.logical_or(first, last)))
+    def _():
+        give_slow()
+
+    @pl.when(last)
+    def _():
+        give_mask(4, 3, 0, (0, 1))
+        for i, pieces in enumerate(FAR):
+            give(x_ref, 4, 0, pieces, far_sem, PIECES + 2 * i, 2, (0, 1))
+        give_rest()
 
     @pl.when(core == 1)
     def _():
         pl.semaphore_wait(ready, 1)
 
-    give_own(1, fast)
+    give_mask(3, 1, 1, fast)
+    for i, pieces in enumerate(NEAR):
+        give(x_ref, 3, core, pieces, near_sem, PIECES + 2 * i, 3, fast)
 
     @pl.when(first)
     def _():
         pl.semaphore_wait(ready, 1)
-        give_own(0, slow)
+        give_slow()
 
     for j in range(3):
         for row, d, at, k in ((0, K, j, j + 2), (1, -1, j + 2, j)):
@@ -158,7 +175,7 @@
                 low[at, k, r, c] = (value - top.astype(F32)).astype(BF16)
                 return carry
 
-            lax.fori_loop(first, first + count, one, 0)
+            lax.fori_loop(first, first + count, one, 0, unroll=count < 3)
 
     dot = functools.partial(jnp.dot, preferred_element_type=F32)
 
@@ -190,7 +207,7 @@
                 out_ref[s] = value * marks[2, pl.ds(s, 1), :]
                 return carry
 
-            lax.fori_loop(first, first + count, one, 0)
+            lax.fori_loop(first, first + count, one, 0, unroll=True)
 
     own.wait()
     own_mask.wait()
@@ -199,24 +216,38 @@
 
     square_row(2, range(5), fresh=True)
 
+    def pass_on(side, i=None):
+        at, far, flip, other = (3, 0, 1 - core, slow) if side else (1, 4, core, fast)
+        if i is None:
+            start(masks.at[at], masks.at[far], mask_sem.at[3 - side], 4 + side, other)
+        else:
+            give(held.at[at], far, flip, FAR[i], far_sem, PIECES * (1 - side) + 2 * i, 6 + side, other)
+
+    def near(side, i):
+        at, flip = (3, 1 - core) if side else (1, core)
+        take(at, flip, NEAR[i], near_sem, PIECES * side + 2 * i)
+        if i < 4 and side:
+            pass_on(side, i)
+        elif i < 4:
+            pl.when(jnp.logical_not(first))(lambda: pass_on(side, i))
+        split(at, flip, NEAR[i], turned=(lambda k: 3 - k) if side else None)
+        if i != 2:
+            k = (3, 2, 1, 1, 0)[i]
+            square_row(at, (4 - k if side else k,))
+
     for side in (1, 0):
-        at, far = (3, 0) if side else (1, 4)
-        flip = 1 - core if side else core
-        other = slow if side else fast
+        at = 3 if side else 1
         landed(masks.at[at], mask_sem.at[side])
-        start(masks.at[at], masks.at[far], mask_sem.at[3 - side], 4 + side, other)
+        if side:
+            pass_on(side)
+        else:
+            pl.when(jnp.logical_not(first))(lambda: pass_on(0))
         mark(at)
-        for i, pieces in enumerate(NEAR):
-            take(at, flip, pieces, near_sem, PIECES * side + 2 * i)
-            if i < len(FAR):
-                give(held.at[at], far, flip, pieces, far_sem, PIECES * (1 - side) + 2 * i, 6 + side, other)
-            split(at, flip, pieces, turned=(lambda k: 3 - k) if side else None)
-            if i != 2:
-                k = (3, 2, 1, 1, 0)[i]
-                square_row(at, (4 - k if side else k,))
-
-    for last in (False, True):
-        side = jnp.where((g == 1) == last, 1, 0)
+        for i in range(5):
+            near(side, i)
+
+    for final in (False, True):
+        side = jnp.where(second == final, 1, 0)
         flip = jnp.where(side == 0, core, 1 - core)
 
         def tile(k, side=side):
@@ -224,13 +255,17 @@
 
         far = tile(0)
         landed(masks.at[far], mask_sem.at[2 + side])
+        if final:
+            pl.when(second)(lambda: start(masks.at[4], masks.at[1], mask_sem.at[0], 8, fast))
         mark(far)
         for i, pieces in enumerate(FAR):
             take(far, flip, pieces, far_sem, PIECES * side + 2 * i)
+            if final:
+                pl.when(second)(lambda: give(held.at[4], 1, 0, pieces, near_sem, 2 * i, 9, fast))
             split(far, flip, pieces, turned=lambda k: tile(k))
             if i == 0:
                 square_row(far, (2,))
-                if last:
+                if final:
                     finish_square(2)
                     cube_row(2, range(5))
             elif i == 1:
@@ -247,7 +282,7 @@
                 for k in (tile(1), tile(2)):
                     cube[k] += product(a_high, a_low, high[far, k, c1, :], low[far, k, c1, :])
                 cube[far, :, c1] += product(a_high, a_low, high[far, far, c1, c1], low[far, far, c1, c1])
-                if last:
+                if final:
                     give_out(flip, ((0, 5, 4), (1, 0, K)), tile)
             else:
                 square[far, r0, c0] += product(high[2, far, r0, :], low[2, far, r0, :], high[far, far, :, c0], low[far, far, :, c0])
@@ -258,14 +293,18 @@
                 k = tile(1)
                 cube[k, r0, :] += product(a_high, a_low, high[far, k, c0, :], low[far, k, c0, :])
                 cube[2, r0, c0] += product(a_high, a_low, high[far, 2, c0, c0], low[far, 2, c0, c0])
-                if last:
+                if final:
                     give_out(flip, ((0, 0, 5),), tile)
 
-    for n in range(2):
-        sent(masks.at[2], n)
-        sent(held.at[2, pl.ds(0, 15)], 2 + n)
-        sent(masks.at[2], 4 + n)
-        sent(held.at[2, pl.ds(0, 11)], 6 + n)
+    def all_sent(first_sem, count):
+        sent(masks.at[2], first_sem)
+        sent(held.at[2, pl.ds(0, count)], first_sem + 1 if first_sem > 7 else first_sem + 2)
+
+    all_sent(0, 15)
+    all_sent(1, 15)
+    all_sent(5, 11)
+    pl.when(jnp.logical_not(first))(lambda: all_sent(4, 11))
+    pl.when(second)(lambda: all_sent(8, 11))
 
 
 def solution(mesh):
@@ -294,7 +333,7 @@
                 pltpu.VMEM((5, TILE, TILE), BF16),
                 pltpu.VMEM((5, TILE, TILE), F32),
                 pltpu.VMEM((5, TILE, TILE), F32),
-                pltpu.SemaphoreType.DMA((8,)),
+                pltpu.SemaphoreType.DMA((10,)),
                 pltpu.SemaphoreType.DMA((4,)),
                 pltpu.SemaphoreType.DMA((2 * PIECES,)),
                 pltpu.SemaphoreType.DMA((2 * PIECES,)),

time: 31.8 us -> 31.2 us (0.981)
  the two profiles are of different devices: /device:TPU:1 before, /device:TPU:48 now
where the time goes in v4:
time: 31.2 us; the launch traced here: 31.1 us
  Pallas kernels  30.1 us (96%)
  local copies, waits for them, and re-layouts  1.02 us (3%)
    pallas_call x1, Pallas kernels, local(): pl.pallas_call(functools.partial(kernel, rows, cols), out_shape=jax.Shape...  30.1 us
    unnamed x1, local copies, waits for them, and re-layouts  1.02 us

profile of v4, /device:TPU:48, one launch (start us, length us, event | category | flops | bytes accessed | tf_op | source)
XLA Modules:
  0.0 31.1 jit_solution(2799740200673129119)
XLA Ops:
  0.0 30.1 %shard_map.28 = f32[18,128,128]{2,1,0:T(8,128)S(1)} custom-call(f32[18,128,128]{2,1,0:T(8,128)} %bitcast.3, s32[2,9]{1,0:T(2,128)} %mask_ref.1), custom_call_target="tpu_custom_call" | custom-call | tf_op jit(solution)/shard_map/pallas_call | solution.py:318
  30.1 1.0 %copy.4 = f32[2,9,128,128]{3,2,1,0:T(8,128)} copy(f32[2,9,128,128]{3,2,1,0:T(8,128)S(1)} %bitcast.2) | data formatting | bytes 2359296

commit v5 on v4

--- a/solution.py
+++ b/solution.py
@@ -20,7 +20,27 @@
 PIECES = 10
 
 
-def kernel(rows, cols, x_ref, mask_ref, out_ref, held, masks, marks, high, low, s_high, s_low, square, cube, send, mask_sem, near_sem, far_sem, local_sem, ready):
+def entry(flip, row, d):
+    s = row * K + d
+    return jnp.where(flip == 0, s, SLOTS - 1 - s)
+
+
+def span(flip, piece):
+    row, d, count = piece
+    s = row * K + d
+    return pl.ds(jnp.where(flip == 0, s, SLOTS - s - count), count)
+
+
+def half(flip, r):
+    return pl.ds(pl.multiple_of(jnp.where(flip == 0, r, 1 - r) * BLK, BLK), BLK)
+
+
+def product(a_high, a_low, b_high, b_low):
+    dot = functools.partial(jnp.dot, preferred_element_type=F32)
+    return dot(a_high, b_high) + (dot(a_high, b_low) + dot(a_low, b_high))
+
+
+def kernel(rows, cols, x_ref, mask_ref, out_ref, marks, high, low, s_high, s_low, square, cube, held, masks, send, mask_sem, near_sem, far_sem, local_sem, ready):
     mine, col = lax.axis_index("row"), lax.axis_index("col")
     core, g = lax.rem(col, 2), mine * cols + col
 
@@ -45,20 +65,6 @@
 
     own = pltpu.make_async_copy(x_ref, held.at[2], local_sem.at[0])
     own_mask = pltpu.make_async_copy(mask_ref, masks.at[2], local_sem.at[1])
-    own.start()
-    own_mask.start()
-
-    def entry(flip, row, d):
-        s = row * K + d
-        return jnp.where(flip == 0, s, SLOTS - 1 - s)
-
-    def span(flip, piece):
-        row, d, count = piece
-        s = row * K + d
-        return pl.ds(jnp.where(flip == 0, s, SLOTS - s - count), count)
-
-    def half(flip, r):
-        return pl.ds(pl.multiple_of(jnp.where(flip == 0, r, 1 - r) * BLK, BLK), BLK)
 
     def place(flip, row, d):
         e = d + row
@@ -136,6 +142,9 @@
         for i, pieces in enumerate(FAR):
             give(x_ref, 4, 0, pieces, far_sem, PIECES + 2 * i, 2, (0, 1))
         give_rest()
+
+    own.start()
+    own_mask.start()
 
     @pl.when(core == 1)
     def _():
@@ -175,12 +184,11 @@
                 low[at, k, r, c] = (value - top.astype(F32)).astype(BF16)
                 return carry
 
-            lax.fori_loop(first, first + count, one, 0, unroll=count < 3)
-
-    dot = functools.partial(jnp.dot, preferred_element_type=F32)
-
-    def product(a_high, a_low, b_high, b_low):
-        return dot(a_high, b_high) + (dot(a_high, b_low) + dot(a_low, b_high))
+            if count < 3:
+                for d in range(first, first + count):
+                    one(d, 0)
+            else:
+                lax.fori_loop(first, first + count, one, 0)
 
     def square_row(j, tiles, fresh=False):
         for k in tiles:
@@ -207,7 +215,8 @@
                 out_ref[s] = value * marks[2, pl.ds(s, 1), :]
                 return carry
 
-            lax.fori_loop(first, first + count, one, 0, unroll=True)
+            for d in range(first, first + count):
+                one(d, 0)
 
     own.wait()
     own_mask.wait()
@@ -284,7 +293,7 @@
                 cube[far, :, c1] += product(a_high, a_low, high[far, far, c1, c1], low[far, far, c1, c1])
                 if final:
                     give_out(flip, ((0, 5, 4), (1, 0, K)), tile)
-            else:
+            elif not final:
                 square[far, r0, c0] += product(high[2, far, r0, :], low[2, far, r0, :], high[far, far, :, c0], low[far, far, :, c0])
                 finish_square(far, r0, c0)
                 a_high, a_low = s_high[far, r0, c0], s_low[far, r0, c0]
@@ -293,8 +302,6 @@
                 k = tile(1)
                 cube[k, r0, :] += product(a_high, a_low, high[far, k, c0, :], low[far, k, c0, :])
                 cube[2, r0, c0] += product(a_high, a_low, high[far, 2, c0, c0], low[far, 2, c0, c0])
-                if final:
-                    give_out(flip, ((0, 0, 5),), tile)
 
     def all_sent(first_sem, count):
         sent(masks.at[2], first_sem)
@@ -307,6 +314,54 @@
     pl.when(second)(lambda: all_sent(8, 11))
 
 
+def finish(cols, part_ref, marks, high, low, s_high, s_low, square, cube, out_ref, rest, sems):
+    g = lax.axis_index("row") * cols + lax.axis_index("col")
+    core, second = lax.rem(g, 2), g == 1
+    flip = jnp.where(second, 1 - core, core)
+    far, near = jnp.where(second, 4, 0), jnp.where(second, 3, 1)
+    copies = []
+
+    def write(source, target, n):
+        copy = pltpu.make_async_copy(source, out_ref.at[target], sems.at[n])
+        copy.start()
+        copies.append(copy)
+
+    for n, piece in enumerate(((1, 0, K), (0, 5, 4))):
+        part = span(flip, piece)
+        write(part_ref.at[part], part, n)
+
+    r0, c0, c1 = half(flip, 0), half(flip, 0), half(flip, 1)
+
+    def times(a, j, k, r, c):
+        return product(*a, high[j, k, r, c], low[j, k, r, c])
+
+    def put(d, at, s_block, c_block):
+        mark = marks[2, pl.ds(entry(flip, 0, d), 1), :]
+        rest[at] = (3.0 * s_block - 2.0 * c_block) * mark
+
+    whole = slice(None)
+    corner = square[far, r0, c0] + times((high[2, far, r0, :], low[2, far, r0, :]), far, far, whole, c0)
+    top = corner.astype(BF16)
+    left = top, (corner - top.astype(F32)).astype(BF16)
+    beside = s_high[far, r0, c1], s_low[far, r0, c1]
+
+    def at(d):
+        return jnp.where(flip == 0, d, 4 - d)
+
+    put(0, at(0), corner, cube[far, r0, c0] + times(left, far, far, c0, c0) + times(beside, far, far, c1, c0))
+    put(1, at(1), square[far, r0, c1], cube[far, r0, c1] + times(left, far, far, c0, c1))
+    both = cube[near, r0, :] + times(left, far, near, c0, whole)
+    for h in range(2):
+        columns = slice(h * BLK, (h + 1) * BLK)
+        d = jnp.where(flip == 0, 2 + h, 3 - h)
+        put(d, at(d), square[near, r0, columns], both[:, columns])
+    put(4, at(4), square[2, r0, c0], cube[2, r0, c0] + times(left, far, 2, c0, c0))
+
+    write(rest, span(flip, (0, 0, 5)), 2)
+    for copy in copies:
+        copy.wait()
+
+
 def solution(mesh):
     rows, cols = mesh.shape["row"], mesh.shape["col"]
 
@@ -315,24 +370,29 @@
             density.reshape(SLOTS, BLK, BLK), pltpu.HBM
         )
         mask = pltpu.with_memory_space_constraint(band_mask, pltpu.HBM)
-        result = pl.pallas_call(
+        tiles, line = (5, 5, TILE, TILE), (5, TILE, TILE)
+        blocks_shape = jax.ShapeDtypeStruct((SLOTS, BLK, BLK), F32)
+        vmem = pl.BlockSpec(memory_space=pltpu.VMEM)
+        parts = pl.pallas_call(
             functools.partial(kernel, rows, cols),
-            out_shape=jax.ShapeDtypeStruct((SLOTS, BLK, BLK), F32),
+            out_shape=[
+                blocks_shape,
+                jax.ShapeDtypeStruct((5, 24, BLK), F32),
+                jax.ShapeDtypeStruct(tiles, BF16),
+                jax.ShapeDtypeStruct(tiles, BF16),
+                jax.ShapeDtypeStruct(line, BF16),
+                jax.ShapeDtypeStruct(line, BF16),
+                jax.ShapeDtypeStruct(line, F32),
+                jax.ShapeDtypeStruct(line, F32),
+            ],
             in_specs=[
                 pl.BlockSpec(memory_space=pltpu.HBM),
                 pl.BlockSpec(memory_space=pltpu.HBM),
             ],
-            out_specs=pl.BlockSpec(memory_space=pltpu.VMEM),
+            out_specs=[vmem] * 8,
             scratch_shapes=[
                 pltpu.VMEM((5, SLOTS, BLK, BLK), F32),
                 pltpu.VMEM((5, 2, K), jnp.int32),
-                pltpu.VMEM((5, 24, BLK), F32),
-                pltpu.VMEM((5, 5, TILE, TILE), BF16),
-                pltpu.VMEM((5, 5, TILE, TILE), BF16),
-                pltpu.VMEM((5, TILE, TILE), BF16),
-                pltpu.VMEM((5, TILE, TILE), BF16),
-                pltpu.VMEM((5, TILE, TILE), F32),
-                pltpu.VMEM((5, TILE, TILE), F32),
                 pltpu.SemaphoreType.DMA((10,)),
                 pltpu.SemaphoreType.DMA((4,)),
                 pltpu.SemaphoreType.DMA((2 * PIECES,)),
@@ -341,9 +401,20 @@
                 pltpu.SemaphoreType.REGULAR,
             ],
             compiler_params=pltpu.CompilerParams(
-                collective_id=0, has_side_effects=True, vmem_limit_bytes=40 << 20
+                collective_id=0, has_side_effects=True, vmem_limit_bytes=24 << 20
             ),
         )(blocks, mask)
+        result = pl.pallas_call(
+            functools.partial(finish, cols),
+            out_shape=blocks_shape,
+            in_specs=[vmem] * 8,
+            out_specs=pl.BlockSpec(memory_space=pltpu.HBM),
+            scratch_shapes=[
+                pltpu.VMEM((5, BLK, BLK), F32),
+                pltpu.SemaphoreType.DMA((3,)),
+            ],
+            compiler_params=pltpu.CompilerParams(vmem_limit_bytes=4 << 20),
+        )(*parts)
         return result.reshape(density.shape)
 
     return jax.shard_map(

time: 31.2 us -> 30.9 us (level)
  the two profiles are of different devices: /device:TPU:48 before, /device:TPU:1 now
where the time goes in v5:
time: 30.9 us; the launch traced here: 30.7 us
  Pallas kernels  30.7 us (99%)
    pallas_call x1, Pallas kernels, local(): pl.pallas_call(functools.partial(kernel, rows, cols), out_shape=[blocks_s...  29.5 us
    pallas_call x1, Pallas kernels, local(): pl.pallas_call(functools.partial(finish, cols), out_shape=blocks_shape, i...  1.25 us

profile of v5, /device:TPU:1, one launch (start us, length us, event | category | flops | bytes accessed | tf_op | source)
XLA Modules:
  0.0 30.7 jit_solution(14106634240732500876)
XLA Ops:
  0.0 29.5 %shard_map.28 = (f32[18,128,128]{2,1,0:T(8,128)S(1)}, f32[5,24,128]{2,1,0:T(8,128)S(1)}, bf16[5,5,256,256]{3,2,1,0:T(8,128)(2,1)S(1)}, bf16[5,5,256,256]{3,2,1,0...) custom-call(f32[18,128,128]{2,1,0:T(8,128)} %bitcast.2, ...), custom_call_target="tpu_custom_call" | custom-call | tf_op jit(solution)/shard_map/pallas_call | solution.py:376
  29.5 1.2 %shard_map.29 = f32[18,128,128]{2,1,0:T(8,128)} custom-call(f32[18,128,128]{2,1,0:T(8,128)S(1)} %get-tuple-element.13.part_ref, f32[5,24,128]{2,1,0:T(8,128)S(1)} %get-tuple-element.14.marks, bf16[5,5,256,256]{3,2,1,0:T(8,128)(2,1)S(1)} %get-tuple-element.15.high, bf16[5,5,256,256]{3,2,1,0:T(8,128)(2,1)S(1)} %get-tuple-element.16.low, ...), custom_call_target="tpu_custom_call" | custom-call | tf_op jit(solution)/shard_map/pallas_call | solution.py:407

commit v6 on v5

--- a/solution.py
+++ b/solution.py
@@ -16,6 +16,7 @@
 
 FAR = ((0, 8, 1), (1, 7, 2)), ((0, 6, 2), (1, 5, 2)), ((0, 5, 1), (1, 4, 1)), ((0, 4, 1), (1, 3, 1))
 NEAR = (*FAR, ((0, 2, 2), (1, 1, 2)))
+MOST = (0, 4, 5), (1, 3, 6)
 
 PIECES = 10
 
@@ -125,8 +126,7 @@
 
     def give_slow():
         give_mask(1, 0, 0, slow)
-        for i, pieces in enumerate(FAR):
-            give(x_ref, 1, 1 - core, pieces, near_sem, 2 * i, 2, slow)
+        give(x_ref, 1, 1 - core, MOST, near_sem, 0, 2, slow)
         give_rest()
 
     def give_rest():
@@ -235,10 +235,8 @@
     def near(side, i):
         at, flip = (3, 1 - core) if side else (1, core)
         take(at, flip, NEAR[i], near_sem, PIECES * side + 2 * i)
-        if i < 4 and side:
+        if i < 4:
             pass_on(side, i)
-        elif i < 4:
-            pl.when(jnp.logical_not(first))(lambda: pass_on(side, i))
         split(at, flip, NEAR[i], turned=(lambda k: 3 - k) if side else None)
         if i != 2:
             k = (3, 2, 1, 1, 0)[i]
@@ -252,7 +250,17 @@
         else:
             pl.when(jnp.logical_not(first))(lambda: pass_on(0))
         mark(at)
-        for i in range(5):
+        if not side:
+            take(1, core, MOST, near_sem, 0)
+
+            @pl.when(jnp.logical_not(first))
+            def _():
+                for i in range(4):
+                    pass_on(0, i)
+
+            split(1, core, MOST)
+            square_row(1, (3, 2, 1))
+        for i in range(5) if side else (4,):
             near(side, i)
 
     for final in (False, True):
@@ -269,8 +277,8 @@
         mark(far)
         for i, pieces in enumerate(FAR):
             take(far, flip, pieces, far_sem, PIECES * side + 2 * i)
-            if final:
-                pl.when(second)(lambda: give(held.at[4], 1, 0, pieces, near_sem, 2 * i, 9, fast))
+            if final and i == 3:
+                pl.when(second)(lambda: give(held.at[4], 1, 0, MOST, near_sem, 0, 9, fast))
             split(far, flip, pieces, turned=lambda k: tile(k))
             if i == 0:
                 square_row(far, (2,))

time: 30.9 us -> 31.7 us (1.026)
  Pallas kernels: 30.7 us -> 31.6 us
    pallas_call x1, Pallas kernels: 29.5 us -> 30.3 us  [local(): pl.pallas_call(functools.partial(kernel, rows, cols), out_shape=[blocks_s...]
where the time goes in v6:
time: 31.7 us; the launch traced here: 31.6 us
  Pallas kernels  31.6 us (100%)
    pallas_call x1, Pallas kernels, local(): pl.pallas_call(functools.partial(kernel, rows, cols), out_shape=[blocks_s...  30.3 us
    pallas_call x1, Pallas kernels, local(): pl.pallas_call(functools.partial(finish, cols), out_shape=blocks_shape, i...  1.25 us

profile of v6, /device:TPU:1, one launch (start us, length us, event | category | flops | bytes accessed | tf_op | source)
XLA Modules:
  0.0 31.6 jit_solution(13915549823773213156)
XLA Ops:
  0.0 30.3 %shard_map.28 = (f32[18,128,128]{2,1,0:T(8,128)S(1)}, f32[5,24,128]{2,1,0:T(8,128)S(1)}, bf16[5,5,256,256]{3,2,1,0:T(8,128)(2,1)S(1)}, bf16[5,5,256,256]{3,2,1,0...) custom-call(f32[18,128,128]{2,1,0:T(8,128)} %bitcast.2, ...), custom_call_target="tpu_custom_call" | custom-call | tf_op jit(solution)/shard_map/pallas_call | solution.py:384
  30.4 1.2 %shard_map.29 = f32[18,128,128]{2,1,0:T(8,128)} custom-call(f32[18,128,128]{2,1,0:T(8,128)S(1)} %get-tuple-element.13.part_ref, f32[5,24,128]{2,1,0:T(8,128)S(1)} %get-tuple-element.14.marks, bf16[5,5,256,256]{3,2,1,0:T(8,128)(2,1)S(1)} %get-tuple-element.15.high, bf16[5,5,256,256]{3,2,1,0:T(8,128)(2,1)S(1)} %get-tuple-element.16.low, ...), custom_call_target="tpu_custom_call" | custom-call | tf_op jit(solution)/shard_map/pallas_call | solution.py:415
